TPU v7x, 256 devices: a whole 4x4x8 slice. The times are simulated.
256 devices in a mesh: row: 16 (over x, z_lo, core), col: 16 (over y, z_hi).
Axes of the slice: x: 4, y: 4, z: 8 (z_hi: 4, z_lo: 2; z = z_hi * 2 + z_lo), core: 2. Of those that a mesh axis runs over, the one named last changes fastest.
Arguments:
- features: bfloat16 [32768, 256], P(('row', 'col')), may hold values from -6 to 6
- degrees: int32 [32768], P(('row', 'col')), may hold values from 256 to 1023
- tile_values: bfloat16 [16, 16, 16, 8, 128, 128], P('row', 'col'), may hold values from 0 to 1
- tile_index: int32 [16, 16, 16, 8], P('row', 'col'), may hold values from 0 to 15, as said below
- tile_count: int32 [16, 16, 16], P('row', 'col'), may hold values from 1 to 8, as said below
- self_weight: bfloat16 [256, 256], replicated, may hold values from -0.375 to 0.375
- neigh_weight: bfloat16 [256, 256], replicated, may hold values from -1.5 to 1.5
- bias: float32 [256], replicated, may hold values from -3 to 3
- out_grad: bfloat16 [32768, 256], P(('row', 'col')), may hold values from -6 to 6
Outputs:
- output: bfloat16 [32768, 256], P(('row', 'col'))
- grad_features: bfloat16 [32768, 256], P(('row', 'col'))
- self_grad: float32 [256, 256], replicated
- neigh_grad: float32 [256, 256], replicated
- bias_grad: float32 [256], replicated
Inputs may be any that keep to these rules, and one draw needn't show every extreme that they name: `tile_index`: within one grid block and column piece the 8 slots name distinct positions. `tile_count`: loads differ between grid blocks; in every draw some column piece has all 8 slots live.
All inputs are finite; a program needn't handle non-finite values.
Results may differ from a plain program's by a relative error of at most 0.012.
Values may be sent and summed in bfloat16 or wider, within the bound.
A program may use at most 128 MiB of HBM per device.

v0:
```python
import jax
import jax.numpy as jnp
from jax import lax
from jax.sharding import PartitionSpec as P


def gelu_tanh(value):
    return jax.nn.gelu(value, approximate=True)


def local(
    features,
    degrees,
    tile_values,
    tile_index,
    tile_count,
    self_weight,
    neigh_weight,
    bias,
    out_grad,
):
    tile_vals = tile_values[0, 0]
    slot_index = tile_index[0, 0]
    slot_count = tile_count[0, 0]
    piece_total = tile_vals.shape[0]
    slot_total = tile_vals.shape[1]
    tile_side = tile_vals.shape[2]
    local_nodes = features.shape[0]
    feat_width = features.shape[1]
    tile_span = local_nodes // tile_side
    rows_tiles = lax.axis_size("col") * local_nodes // tile_side
    tile_rows = slot_index // tile_span
    tile_cols = slot_index % tile_span
    live_slots = jnp.arange(slot_total, dtype=jnp.int32)[None, :] < slot_count[:, None]
    masked = jnp.where(live_slots[:, :, None, None], tile_vals, jnp.zeros((), tile_vals.dtype))
    column_feats = lax.all_gather(features, "row", axis=0, tiled=True).reshape(
        piece_total, tile_span, tile_side, feat_width
    )
    source = column_feats[jnp.arange(piece_total, dtype=jnp.int32)[:, None], tile_cols]
    product = jnp.einsum("pkab,pkbf->pkaf", masked, source, preferred_element_type=jnp.float32)
    flat_products = product.reshape(-1, tile_side, feat_width)
    flat_keys = tile_rows.reshape(-1)
    row_total = rows_tiles * tile_side
    span_tiles = row_total // tile_side
    keys = flat_keys - 0 // tile_side
    inside = (keys >= 0) & (keys < span_tiles)
    keys = jnp.where(inside, keys, span_tiles)
    summed = jax.ops.segment_sum(flat_products, keys, num_segments=span_tiles + 1)
    aggregate = lax.psum_scatter(
        summed[:span_tiles].reshape(row_total, feat_width), "col", scatter_dimension=0, tiled=True
    )
    inverse = 1.0 / degrees.astype(jnp.float32)
    neighbour_mean = (aggregate * inverse[:, None]).astype(jnp.bfloat16)
    preact = jnp.dot(features, self_weight, preferred_element_type=jnp.float32)
    preact = (
        preact + jnp.dot(neighbour_mean, neigh_weight, preferred_element_type=jnp.float32) + bias
    )
    activated, grad_fn = jax.vjp(gelu_tanh, preact)
    output = activated.astype(jnp.bfloat16)
    (grad_pre,) = grad_fn(out_grad.astype(jnp.float32))
    grad_preact = grad_pre.astype(jnp.bfloat16)
    node_dims = (((0,), (0,)), ((), ()))
    self_part = lax.dot_general(
        features, grad_preact, node_dims, preferred_element_type=jnp.float32
    )
    neigh_part = lax.dot_general(
        neighbour_mean, grad_preact, node_dims, preferred_element_type=jnp.float32
    )
    bias_part = jnp.sum(grad_preact.astype(jnp.float32), axis=0)
    self_grad, neigh_grad, bias_grad = lax.psum((self_part, neigh_part, bias_part), ("row", "col"))
    out_dims = (((1,), (1,)), ((), ()))
    scaled_grad = (
        lax.dot_general(grad_preact, neigh_weight, out_dims, preferred_element_type=jnp.float32)
        * inverse[:, None]
    ).astype(jnp.bfloat16)
    grad_rows = lax.all_gather(scaled_grad, "col", axis=0, tiled=True).reshape(
        rows_tiles, tile_side, feat_width
    )
    source = grad_rows[tile_rows]
    product = jnp.einsum("pkab,pkaf->pkbf", masked, source, preferred_element_type=jnp.float32)
    seg_keys = jnp.arange(piece_total, dtype=jnp.int32)[:, None] * tile_span + tile_cols
    back_part = jax.ops.segment_sum(
        product.reshape(-1, tile_side, feat_width),
        seg_keys.reshape(-1),
        num_segments=piece_total * tile_span,
    )
    back_sum = lax.psum_scatter(
        back_part.reshape(piece_total * local_nodes, feat_width).astype(jnp.bfloat16),
        "row",
        scatter_dimension=0,
        tiled=True,
    ).astype(jnp.float32)
    grad_features = (
        lax.dot_general(grad_preact, self_weight, out_dims, preferred_element_type=jnp.float32)
        + back_sum
    ).astype(jnp.bfloat16)
    return (output, grad_features, self_grad, neigh_grad, bias_grad)


def solution(mesh):
    placed = (
        P(("row", "col"), None),
        P(("row", "col")),
        P("row", "col", None, None, None, None),
        P("row", "col", None, None),
        P("row", "col", None),
        P(),
        P(),
        P(),
        P(("row", "col"), None),
    )
    return jax.shard_map(
        local,
        mesh=mesh,
        in_specs=placed,
        out_specs=(P(("row", "col"), None), P(("row", "col"), None), P(), P(), P()),
        check_vma=False,
    )
```

profile of v0, /device:TPU:1, one launch (start us, length us, event | category | flops | bytes accessed | tf_op | source)
XLA Modules:
  0.0 567.7 jit_solution(1255715857694155963)
XLA Ops:
  7.2 0.0 copy-start
  7.2 0.0 all-gather.3.cloned.1.call-start
  7.2 0.7 all-gather.3.cloned.1.call-update
  7.9 0.0 reduce-scatter.3.cloned.1.call-start
  8.0 0.8 copy.18
  8.7 0.1 squeeze.8
  8.8 0.7 iota_compare_fusion
  9.6 39.6 %all-gather.3.cloned.1.call-done = bf16[2048,256]{1,0:T(8,128)(2,1)} async-done(((bf16[128,256]{1,0:T(8,128)(2,1)}), bf16[2048,256]{1,0:T(8,128)(2,1)}) %all-gather.3.cloned.1.call-update) | async-done | bytes 1048592 | tf_op jit(solution)/shard_map/all_gather | solution.py:36
  49.1 8.1 %gather_fusion = bf16[128,128,256]{2,1,0:T(8,128)(2,1)} fusion(bf16[16,1,128,256]{3,2,0,1:T(8,128)(2,1)} %bitcast.37, s32[128]{0:T(128)} %constant.85), kind=kCustom, calls=%fused_computation | custom fusion | bytes 16778240 | tf_op jit(solution)/shard_map/gather | solution.py:39
  57.2 12.8 %fusion.1 = f32[16,8,128,256]{3,2,1,0:T(8,128)} fusion(bf16[16,8,128,256]{3,2,1,0:T(8,128)(2,1)} %bitcast.40, bf16[1,1,16,8,128,128]{5,4,3,2,1,0:T(8,128)(2,1)} %param.11, pred[16,8]{1,0:T(8,128)(4,1)S(1)} %iota_compare_fusion), kind=kOutput, calls=%fused_computation.6 | convolution fusion | flops 1075838976 | bytes 29360256 | tf_op jit(solution)/shard_map/pkab,pkbf->pkaf/dot_general | solution.py:40
  70.0 0.2 broadcast_in_dim.17
  70.2 0.0 copy-start.6
  70.2 0.0 copy-start.1
  70.2 0.0 copy-start.2
  70.2 0.0 copy-start.4
  70.2 0.0 copy-start.5
  70.2 0.0 copy-start.3
  70.3 24.4 %scatter_fusion = f32[17,128,256]{2,1,0:T(8,128)S(1)} fusion(f32[17,128,256]{2,1,0:T(8,128)S(1)} %broadcast_in_dim.17, s32[128]{0:T(128)S(1)} %fusion.17, f32[128,128,256]{2,1,0:T(8,128)} %bitcast.36), kind=kCustom, calls=%fused_computation.2 | custom fusion | flops 4194304 | bytes 50332160 | tf_op jit(solution)/shard_map/scatter-add | solution.py:48
  94.7 1.5 slice.8
  96.2 0.0 reduce-scatter.3.cloned.1.call-update
  96.2 0.0 all-gather.5.cloned.1.call-start
  96.3 0.0 copy-done.6
  96.3 0.2 fusion.22
  96.5 86.4 %reduce-scatter.3.cloned.1.call-done = f32[128,256]{1,0:T(8,128)} async-done(((f32[2048,256]{1,0:T(8,128)}), f32[128,256]{1,0:T(8,128)}) %reduce-scatter.3.cloned.1.call-update) | async-done | bytes 131088 | tf_op jit(solution)/shard_map/reduce_scatter | solution.py:49
  182.9 1.8 convert_reduce_fusion
  184.8 0.8 fusion.6
  185.6 0.0 all-gather.5.cloned.1.call-update
  185.6 0.0 all-reduce.3.cloned.1.call-start
  185.7 0.1 copy.19
  185.8 0.1 reshape.138
  185.9 0.1 reshape.154
  186.0 0.9 convolution_bitcast_fusion
  186.9 1.9 fusion.20
  188.8 0.0 all-reduce.3.cloned.1.call-update
  188.8 0.2 reduce-scatter.5.cloned.1.call-start
  189.0 48.6 %all-gather.5.cloned.1.call-done = bf16[2048,256]{1,0:T(8,128)(2,1)} async-done(((bf16[128,256]{1,0:T(8,128)(2,1)}), bf16[2048,256]{1,0:T(8,128)(2,1)}) %all-gather.5.cloned.1.call-update) | async-done | bytes 1048592 | tf_op jit(solution)/shard_map/all_gather | solution.py:76
  237.6 7.8 %gather_fusion.1 = bf16[128,128,256]{2,1,0:T(8,128)(2,1)} fusion(bf16[16,128,256]{2,1,0:T(8,128)(2,1)} %bitcast.38, s32[1024]{0:T(1024)S(1)} %pad_clamp_fusion), kind=kCustom, calls=%fused_computation.1 | custom fusion | bytes 16777728 | tf_op jit(solution)/shard_map/gather | solution.py:79
  245.4 13.9 %fusion = f32[16,8,128,256]{3,2,1,0:T(8,128)} fusion(bf16[16,8,128,256]{3,2,1,0:T(8,128)(2,1)} %bitcast.39, bf16[1,1,16,8,128,128]{5,4,3,2,1,0:T(8,128)(2,1)} %param.11, pred[16,8]{1,0:T(8,128)(4,1)S(1)} %iota_compare_fusion), kind=kOutput, calls=%fused_computation.5 | convolution fusion | flops 1075838976 | bytes 29360256 | tf_op jit(solution)/shard_map/pkab,pkaf->pkbf/dot_general | solution.py:80
  259.3 0.2 broadcast_in_dim.21
  259.5 24.1 %scatter_fusion.1 = f32[16,128,256]{2,1,0:T(8,128)S(1)} fusion(f32[16,128,256]{2,1,0:T(8,128)S(1)} %broadcast_in_dim.21, s32[128]{0:T(128)S(1)} %reshape.154, f32[128,128,256]{2,1,0:T(8,128)} %bitcast.35), kind=kCustom, calls=%fused_computation.3 | custom fusion | flops 4194304 | bytes 50332160 | tf_op jit(solution)/shard_map/scatter-add | solution.py:82
  283.6 1.1 convert_element_type.39
  284.7 0.0 reduce-scatter.5.cloned.1.call-update
  284.7 75.5 %psum.23 = f32[256]{0:T(256)} all-reduce(f32[256]{0:T(256)S(1)} %get-tuple-element.17), channel_id=1, replica_groups=mesh['row'=16,'col'=16] {'row','col'}, use_global_device_ids=true, to_apply=%region_7.8 | all-reduce | flops 256 | bytes 2048 | tf_op jit(solution)/shard_map/psum | solution.py:70
  360.2 133.9 %all-reduce.3.cloned.1.call-done = (f32[256,256]{0,1:T(8,128)}, f32[256,256]{1,0:T(8,128)}) async-done(((f32[256,256]{0,1:T(8,128)}, f32[256,256]{1,0:T(8,128)}), (f32[256,256]{0,1:T(8,128)}, f32[256,256]{1,0:T(8,128)})) %all-reduce.3.cloned.1.call-update) | async-done | bytes 524304 | tf_op jit(solution)/shard_map/psum | solution.py:70
  494.2 1.8 copy.21
  496.0 61.9 %reduce-scatter.5.cloned.1.call-done = bf16[128,256]{1,0:T(8,128)(2,1)} async-done(((bf16[2048,256]{1,0:T(8,128)(2,1)}), bf16[128,256]{1,0:T(8,128)(2,1)}) %reduce-scatter.5.cloned.1.call-update) | async-done | bytes 65552 | tf_op jit(solution)/shard_map/reduce_scatter | solution.py:87
  557.8 1.7 fusion.5
  559.5 1.7 copy.27
  (11 shorter events, 0.0 us)
Async XLA Ops:
  7.2 175.8 %copy-start = (bf16[256,256]{1,0:T(8,128)(2,1)S(1)}, bf16[256,256]{1,0:T(8,128)(2,1)}, u32[]{:S(2)}) copy-start(bf16[256,256]{1,0:T(8,128)(2,1)} %param.15) | copy-start | bytes 393220
  7.2 41.9 %all-gather.3.cloned.1.call-start = ((), (), s32[]{:S(2)}) async-start(), calls=%async_computation.2 | async-start | bytes 1114112 | tf_op jit(solution)/shard_map/all_gather | solution.py:36
  7.9 175.0 %reduce-scatter.3.cloned.1.call-start = ((), (), s32[]{:S(2)}) async-start(), calls=%async_computation.3 | async-start | bytes 2228224 | tf_op jit(solution)/shard_map/reduce_scatter | solution.py:49
  70.2 26.1 %copy-start.6 = (s32[128]{0:T(128)S(1)}, s32[128]{0:T(128)}, u32[]{:S(2)}) copy-start(s32[128]{0:T(128)} %param.10) | copy-start | bytes 1540
  70.2 26.1 %copy-start.1 = (bf16[128,256]{1,0:T(8,128)(2,1)S(1)}, bf16[128,256]{1,0:T(8,128)(2,1)}, u32[]{:S(2)}) copy-start(bf16[128,256]{1,0:T(8,128)(2,1)} %param.9) | copy-start | bytes 196612
  70.2 26.1 %copy-start.2 = (bf16[256,256]{1,0:T(8,128)(2,1)S(1)}, bf16[256,256]{1,0:T(8,128)(2,1)}, u32[]{:S(2)}) copy-start(bf16[256,256]{1,0:T(8,128)(2,1)} %param.14) | copy-start | bytes 393220
  70.2 112.7 %copy-start.4 = (bf16[128,256]{1,0:T(8,128)(2,1)S(1)}, bf16[128,256]{1,0:T(8,128)(2,1)}, u32[]{:S(2)}) copy-start(bf16[128,256]{1,0:T(8,128)(2,1)} %param.17) | copy-start | bytes 196612
  70.2 112.7 %copy-start.5 = (f32[256]{0:T(256)S(1)}, f32[256]{0:T(256)}, u32[]{:S(2)}) copy-start(f32[256]{0:T(256)} %param.16) | copy-start | bytes 3076
  70.2 115.4 %copy-start.3 = (s32[1,1,16,8]{2,3,1,0:T(8,128)S(1)}, s32[1,1,16,8]{2,3,1,0:T(8,128)}, u32[]{:S(2)}) copy-start(s32[1,1,16,8]{2,3,1,0:T(8,128)} %param.12) | copy-start | bytes 1540
  96.2 141.4 %all-gather.5.cloned.1.call-start = ((), (), s32[]{:S(2)}) async-start(), calls=%async_computation.4 | async-start | bytes 1114112 | tf_op jit(solution)/shard_map/all_gather | solution.py:76
  185.6 308.5 %all-reduce.3.cloned.1.call-start = ((), (), s32[]{:S(2)}) async-start(), calls=%async_computation.6 | async-start | bytes 1048576 | tf_op jit(solution)/shard_map/psum | solution.py:70
  188.8 369.0 %reduce-scatter.5.cloned.1.call-start = ((), (), s32[]{:S(2)}) async-start(), calls=%async_computation.5 | async-start | bytes 1114112 | tf_op jit(solution)/shard_map/reduce_scatter | solution.py:87
Sparse Core Ops, SparseCore 0:
  9.9 39.1 all-gather.2
  96.4 86.5 reduce-scatter.2
  186.2 51.3 all-gather.4
  244.6 249.4 all-reduce.2
  496.7 61.0 reduce-scatter.4
where the time goes:
time: 571 us; the launch traced here: 568 us
  waiting for transfers between devices  371 us (65%)
  blocking collectives  75.5 us (13%)
  other arithmetic  50.3 us (9%)
  matrix products  34 us (6%)
  local copies, waits for them, and re-layouts  22.4 us (4%)
  between operations  14 us (2%)
    psum x1, waiting for transfers between devices, local(): lax.psum((self_part, neigh_part, bias_part), ('row', 'col'))  134 us
    reduce_scatter x1, waiting for transfers between devices, local(): lax.psum_scatter(summed[:span_tiles].reshape(row_total, feat_width), 'col...  86.4 us
    psum x1, blocking collectives, local(): lax.psum((self_part, neigh_part, bias_part), ('row', 'col'))  75.5 us
    reduce_scatter x1, waiting for transfers between devices, local(): lax.psum_scatter(back_part.reshape(piece_total * local_nodes, feat_width)...  61.9 us
    all_gather x1, waiting for transfers between devices, local(): lax.all_gather(scaled_grad, 'col', axis=0, tiled=True)  48.6 us
    all_gather x1, waiting for transfers between devices, local(): lax.all_gather(features, 'row', axis=0, tiled=True)  39.6 us
    scatter-add x1, other arithmetic, local(): jax.ops.segment_sum(flat_products, keys, num_segments=span_tiles + 1)  24.4 us
    scatter-add x1, other arithmetic, local(): jax.ops.segment_sum(product.reshape(-1, tile_side, feat_width), seg_keys....  24.1 us
  transfers between devices with their start and end apart: 5, of which 5 were waited for; matrix products, arithmetic and copies ran while one was open for 9% of the time, Pallas kernels for 0%

commit v1 on v0

v1 whole, which is shorter than its diff:
```python
import functools

import jax
import jax.numpy as jnp
from jax import lax
from jax.experimental import pallas as pl
from jax.experimental.pallas import tpu as pltpu
from jax.sharding import PartitionSpec as P

MESH = pl.DeviceIdType.MESH
F32 = jnp.float32
BF16 = jnp.bfloat16
T = 128
W = 256
CHIPS = [(dx, dz) for dx in (2, 1, 3, 0) for dz in (1, 0) if dx or dz]
PLANE = [(dx, dy) for dx in range(4) for dy in range(4) if dx or dy]
FAR = (2, 1, 3)
GELU_C = 0.7978845608028654


def dot(lhs, rhs, lhs_dim=1, rhs_dim=0):
    return lax.dot_general(
        lhs, rhs, (((lhs_dim,), (rhs_dim,)), ((), ())), preferred_element_type=F32
    )


def device(x, zl, c, y, zh):
    return (x * 4 + zl * 2 + c, y * 4 + zh)


def split_rows(total):
    high = total.astype(BF16).astype(F32)
    return high, total - high


def bias_block(total):
    high, low = split_rows(total)
    line = lax.broadcasted_iota(jnp.int32, (16, W), 0)
    return jnp.where(line == 0, high, jnp.where(line == 1, low, 0.0)).astype(BF16)


def kernel(
    slot_s, feats_h, deg_h, tiles_h, ws_h, wn_h, bias_h, og_h,
    out_h, gf_h, sg_h, ng_h, bg_h,
    tiles, tiles_t, dense, dense_t, feats_all, grads_all, deg_v, ws, wn, bias_v, og_v,
    base, recip, part_b, recv_by, sum_z, recv_bz, gp_v, nm_v, out_v, gf_v, self_keep,
    part_d, recv_ds, sum_d, recv_d,
    ar1_s, ar1_r, ar2_s, ar2_r, ar3_s, ar3_r, ar4, ar5_r, sg_v, ng_v, bg_v,
    local_sem, a_ss, a_rs, af_ss, af_rs, by_ss, by_rs, bz_ss, bz_rs,
    cz_ss, cz_rs, cy_ss, cy_rs, ds_ss, ds_rs, d_ss, d_rs,
    r1_ss, r1_rs, r2_ss, r2_rs, r3_ss, r3_rs, r4_ss, r4_rs, r5_ss, r5_rs,
):
    a = lax.axis_index("row")
    b = lax.axis_index("col")
    x, zl, c = a // 4, (a // 2) % 2, a % 2
    y, zh = b // 4, b % 4
    z = zh * 2 + zl
    sib = device(x, zl, 1 - c, y, zh)
    sent = []

    def send(src, dst, send_sem, recv_sem, where):
        copy = pltpu.make_async_remote_copy(
            src_ref=src, dst_ref=dst, send_sem=send_sem, recv_sem=recv_sem,
            device_id=where, device_id_type=MESH,
        )
        copy.start()
        sent.append(copy)
        return copy

    def chip(dx, dz):
        return (x + dx) % 4, (zl + dz) % 2

    loads = [
        pltpu.make_async_copy(feats_h, feats_all.at[a], local_sem.at[0]),
        pltpu.make_async_copy(tiles_h, tiles, local_sem.at[1]),
        pltpu.make_async_copy(ws_h, ws, local_sem.at[2]),
        pltpu.make_async_copy(wn_h, wn, local_sem.at[3]),
        pltpu.make_async_copy(bias_h, bias_v, local_sem.at[4]),
        pltpu.make_async_copy(og_h, og_v, local_sem.at[5]),
        pltpu.make_async_copy(deg_h, deg_v, local_sem.at[6]),
    ]
    for load in loads:
        load.start()

    partners = [sib]
    partners += [device(*chip(dx, dz), c, y, zh) for dx, dz in CHIPS]
    partners += [device((x + dx) % 4, zl, c, (y + dy) % 4, zh) for dx, dy in PLANE if dy]
    partners += [
        device(x, zz % 2, c, y, zz // 2)
        for zz in [(z + d) % 8 for d in range(1, 8)]
    ]
    barrier = pltpu.get_barrier_semaphore()
    for partner in partners:
        pl.semaphore_signal(barrier, inc=1, device_id=partner, device_id_type=MESH)
    pl.semaphore_wait(barrier, len(partners))

    own_to_sib = send(feats_h, feats_all.at[a], a_ss.at[7], a_rs.at[7], sib)
    a_sent = []
    for j, (dx, dz) in enumerate(CHIPS):
        where = device(*chip(dx, dz), c, y, zh)
        a_sent.append(send(feats_h, feats_all.at[a], a_ss.at[j], a_rs.at[j], where))

    for load in loads:
        load.wait()

    def build(q, carry):
        r = (q % 4) * 4 + q // 4
        for p in range(16):
            slot = slot_s[p, r]
            tile = tiles[p * 8 + jnp.minimum(slot, 7)]
            dense[q, :, p * T : (p + 1) * T] = jnp.where(slot < 8, tile, jnp.zeros_like(tile))
        return carry

    lax.fori_loop(0, 16, build, 0)
    base[...] = dot(feats_all[a], ws[...]) + bias_v[...]
    inverse = jnp.broadcast_to(1.0 / deg_v[...].astype(F32), (T, T)).T
    recip[...] = jnp.concatenate([inverse, inverse], axis=1)

    forwards = []
    for j in (4, 1, 3, 5, 6, 0, 2):
        dx, dz = CHIPS[j]
        a_sent[j].wait_recv()
        px, pz = chip(-dx, dz)
        piece = px * 4 + pz * 2 + c
        forwards.append(
            send(feats_all.at[piece], feats_all.at[piece], af_ss.at[j], af_rs.at[j], sib)
        )
    own_to_sib.wait_recv()
    for copy in forwards:
        copy.wait_recv()

    gathered = feats_all[...].reshape(16 * T, W)
    by_sent = []
    for i, dz in enumerate((2, 1, 3, 0)):
        zz = (zh + dz) % 4
        part = dot(dense[pl.ds(zz * 4, 4)].reshape(4 * T, 16 * T), gathered)
        part_b[i] = part.reshape(4, T, W).astype(BF16)
        row = []
        for k, dy in enumerate(FAR):
            yy = (y + dy) % 4
            row.append(
                send(
                    part_b.at[i, yy], recv_by.at[i, k], by_ss.at[i, k], by_rs.at[i, k],
                    device(x, zl, c, yy, zh),
                )
            )
        by_sent.append(row)

    def transpose(p, carry):
        for k in range(8):
            tiles_t[p * 8 + k] = tiles[p * 8 + k].T
        return carry

    lax.fori_loop(0, 16, transpose, 0)

    bz_sent = []
    own = None
    for i, dz in enumerate((2, 1, 3, 0)):
        total = part_b[i, y].astype(F32)
        for k in range(3):
            by_sent[i][k].wait_recv()
            total = total + recv_by[i, k].astype(F32)
        if dz:
            sum_z[i] = total.astype(BF16)
            bz_sent.append(
                send(
                    sum_z.at[i], recv_bz.at[i], bz_ss.at[i], bz_rs.at[i],
                    device(x, zl, c, y, (zh + dz) % 4),
                )
            )
        else:
            own = total

    def build_t(p, carry):
        place = (p // 4) * 4 + (p % 2) * 2 + (p // 2) % 2
        for q in range(16):
            r = (q % 4) * 4 + q // 4
            slot = slot_s[p, r]
            tile = tiles_t[p * 8 + jnp.minimum(slot, 7)]
            dense_t[place, :, q * T : (q + 1) * T] = jnp.where(
                slot < 8, tile, jnp.zeros_like(tile)
            )
        return carry

    lax.fori_loop(0, 16, build_t, 0)

    for i in range(3):
        bz_sent[i].wait_recv()
        own = own + recv_bz[i].astype(F32)

    inverse = recip[...]
    mean = (own * inverse).astype(BF16)
    pre = base[...] + dot(mean, wn[...])
    tanh = jnp.tanh(GELU_C * (pre + 0.044715 * (pre * pre * pre)))
    slope = 0.5 * (1.0 + tanh) + 0.5 * pre * (1.0 - tanh * tanh) * (
        GELU_C * (1.0 + 3.0 * 0.044715 * (pre * pre))
    )
    gp = (og_v[...].astype(F32) * slope).astype(BF16)
    me = zh * 4 + y
    grads_all[me] = (dot(gp, wn[...], 1, 1) * inverse).astype(BF16)

    cz_sent = []
    cy_sent = []
    for k, d in enumerate(FAR):
        cz_sent.append(
            send(
                grads_all.at[me], grads_all.at[me], cz_ss.at[k], cz_rs.at[k],
                device(x, zl, c, y, (zh + d) % 4),
            )
        )
    for k, d in enumerate(FAR):
        cy_sent.append(
            send(
                grads_all.at[me], grads_all.at[me], cy_ss.at[3, k], cy_rs.at[3, k],
                device(x, zl, c, (y + d) % 4, zh),
            )
        )

    out_v[...] = (0.5 * pre * (1.0 + tanh)).astype(BF16)
    store_out = pltpu.make_async_copy(out_v, out_h, local_sem.at[7])
    store_out.start()

    self_part = dot(feats_all[a], gp, 0, 0)
    neigh_part = dot(mean, gp, 0, 0)
    bias_part = jnp.sum(gp.astype(F32), axis=0, keepdims=True)
    first = c == 0
    ar1_s[0:W] = jnp.where(first, neigh_part, self_part).astype(BF16)
    ar1_s[W : W + 16] = bias_block(bias_part)
    r1 = send(ar1_s, ar1_r, r1_ss, r1_rs, sib)
    keep = jnp.where(first, self_part, neigh_part)
    self_keep[...] = dot(gp, ws[...], 1, 1)
    r1.wait_recv()
    chunk = keep + ar1_r[0:W].astype(F32)
    ar2_s[:, 0:16] = chunk.reshape(16, 16, W).astype(BF16)
    other = ar1_r[W : W + 16].astype(F32)
    mine = ar1_s[W : W + 16].astype(F32)
    both = jnp.sum(mine + other, axis=0, keepdims=True)
    ar2_s[:, 16:32] = jnp.broadcast_to(bias_block(both)[None], (16, 16, W))
    spot = x * 4 + y
    r2 = []
    for j, (dx, dy) in enumerate(PLANE):
        xx, yy = (x + dx) % 4, (y + dy) % 4
        r2.append(
            send(
                ar2_s.at[xx * 4 + yy], ar2_r.at[spot], r2_ss.at[j], r2_rs.at[j],
                device(xx, zl, c, yy, zh),
            )
        )
    ar2_r[spot] = ar2_s[spot]

    for k in (1, 2, 0):
        d = FAR[k]
        cz_sent[k].wait_recv()
        piece = ((zh - d) % 4) * 4 + y
        for m, dy in enumerate(FAR):
            cy_sent.append(
                send(
                    grads_all.at[piece], grads_all.at[piece], cy_ss.at[k, m], cy_rs.at[k, m],
                    device(x, zl, c, (y + dy) % 4, zh),
                )
            )

    for copy in r2:
        copy.wait_recv()
    total = jnp.zeros((32, W), F32)
    for j in range(16):
        total = total + ar2_r[j].astype(F32)
    ar3_s[0:16] = total[0:16].astype(BF16)
    ar3_s[16:32] = bias_block(jnp.sum(total[16:32], axis=0, keepdims=True))
    r3 = []
    for j in range(7):
        zz = (z + j + 1) % 8
        r3.append(
            send(
                ar3_s, ar3_r.at[z], r3_ss.at[j], r3_rs.at[j], device(x, zz % 2, c, y, zz // 2)
            )
        )
    ar3_r[z] = ar3_s[...]

    for copy in cy_sent:
        copy.wait_recv()

    grads = grads_all[...].reshape(16 * T, W)
    ds_sent = []
    for i, dx in enumerate((2, 1, 3, 0)):
        xx = (x + dx) % 4
        part = dot(dense_t[pl.ds(xx * 4, 4)].reshape(4 * T, 16 * T), grads)
        part_d[i] = part.reshape(2, 2, T, W).astype(BF16)
        ds_sent.append(send(part_d.at[i, 1 - c], recv_ds.at[i], ds_ss.at[i], ds_rs.at[i], sib))

    d_sent = []
    back = None
    for i, dx in enumerate((2, 1, 3, 0)):
        ds_sent[i].wait_recv()
        total = part_d[i, c].astype(F32) + recv_ds[i].astype(F32)
        sum_d[i] = total.astype(BF16)
        for dz in (1, 0):
            if dx or dz:
                xx, zz = chip(dx, dz)
                j = CHIPS.index((dx, dz))
                d_sent.append(
                    send(
                        sum_d.at[i, zz], recv_d.at[j], d_ss.at[j], d_rs.at[j],
                        device(xx, zz, c, y, zh),
                    )
                )
    back = self_keep[...] + sum_d[3, zl].astype(F32)

    for copy in r3:
        copy.wait_recv()
    total = jnp.zeros((32, W), F32)
    for j in range(8):
        total = total + ar3_r[j].astype(F32)
    bg_v[...] = jnp.sum(total[16:32], axis=0, keepdims=True)
    ar4[spot] = total[0:16].astype(BF16)
    r4 = []
    for j, (dx, dy) in enumerate(PLANE):
        xx, yy = (x + dx) % 4, (y + dy) % 4
        r4.append(
            send(
                ar4.at[spot], ar4.at[spot], r4_ss.at[j], r4_rs.at[j], device(xx, zl, c, yy, zh)
            )
        )
    for copy in r4:
        copy.wait_recv()
    r5 = send(ar4, ar5_r, r5_ss, r5_rs, sib)

    for copy in d_sent:
        copy.wait_recv()
    for j in range(7):
        back = back + recv_d[j].astype(F32)
    gf_v[...] = back.astype(BF16)
    store_gf = pltpu.make_async_copy(gf_v, gf_h, local_sem.at[8])
    store_gf.start()

    r5.wait_recv()
    here = ar4[...].reshape(W, W).astype(F32)
    there = ar5_r[...].reshape(W, W).astype(F32)
    sg_v[...] = jnp.where(first, here, there)
    ng_v[...] = jnp.where(first, there, here)
    stores = [
        store_out,
        store_gf,
        pltpu.make_async_copy(sg_v, sg_h, local_sem.at[9]),
        pltpu.make_async_copy(ng_v, ng_h, local_sem.at[10]),
        pltpu.make_async_copy(bg_v, bg_h, local_sem.at[11]),
    ]
    for store in stores[2:]:
        store.start()
    for store in stores:
        store.wait()
    for copy in sent:
        copy.wait_send()


def local(
    features, degrees, tile_values, tile_index, tile_count, self_weight, neigh_weight, bias,
    out_grad,
):
    index = tile_index[0, 0]
    count = tile_count[0, 0]
    slots = jnp.arange(8, dtype=jnp.int32)
    live = slots[None, :] < count[:, None]
    match = (index[:, :, None] == jnp.arange(16, dtype=jnp.int32)) & live[:, :, None]
    slot = jnp.min(jnp.where(match, slots[None, :, None], 8), axis=1)

    vm = pltpu.VMEM
    dma = pltpu.SemaphoreType.DMA
    anywhere = pl.BlockSpec(memory_space=pl.ANY)
    scratch = [
        vm((128, T, T), BF16), vm((128, T, T), BF16),
        vm((16, T, 16 * T), BF16), vm((16, T, 16 * T), BF16),
        vm((16, T, W), BF16), vm((16, T, W), BF16),
        vm((1, T), jnp.int32), vm((W, W), BF16), vm((W, W), BF16), vm((1, W), F32),
        vm((T, W), BF16),
        vm((T, W), F32), vm((T, W), F32),
        vm((4, 4, T, W), BF16), vm((4, 3, T, W), BF16), vm((3, T, W), BF16),
        vm((3, T, W), BF16),
        vm((T, W), BF16), vm((T, W), BF16), vm((T, W), BF16), vm((T, W), BF16), vm((T, W), F32),
        vm((4, 2, 2, T, W), BF16), vm((4, 2, T, W), BF16), vm((4, 2, T, W), BF16),
        vm((7, T, W), BF16),
        vm((W + 16, W), BF16), vm((W + 16, W), BF16),
        vm((16, 32, W), BF16), vm((16, 32, W), BF16),
        vm((32, W), BF16), vm((8, 32, W), BF16),
        vm((16, 16, W), BF16), vm((16, 16, W), BF16),
        vm((W, W), F32), vm((W, W), F32), vm((1, W), F32),
        dma((12,)), dma((8,)), dma((8,)), dma((7,)), dma((7,)),
        dma((4, 3)), dma((4, 3)), dma((3,)), dma((3,)),
        dma((3,)), dma((3,)), dma((4, 3)), dma((4, 3)),
        dma((4,)), dma((4,)), dma((7,)), dma((7,)),
        dma(()), dma(()), dma((15,)), dma((15,)), dma((7,)), dma((7,)),
        dma((15,)), dma((15,)), dma(()), dma(()),
    ]
    output, grad_features, self_grad, neigh_grad, bias_grad = pl.pallas_call(
        kernel,
        out_shape=(
            jax.ShapeDtypeStruct((T, W), BF16),
            jax.ShapeDtypeStruct((T, W), BF16),
            jax.ShapeDtypeStruct((W, W), F32),
            jax.ShapeDtypeStruct((W, W), F32),
            jax.ShapeDtypeStruct((1, W), F32),
        ),
        in_specs=[pl.BlockSpec(memory_space=pltpu.SMEM)] + [anywhere] * 7,
        out_specs=[anywhere] * 5,
        scratch_shapes=scratch,
        compiler_params=pltpu.CompilerParams(
            collective_id=0, has_side_effects=True, vmem_limit_bytes=56 * 2**20
        ),
        name="sage",
    )(
        slot,
        features,
        degrees.reshape(1, T),
        tile_values.reshape(128, T, T),
        self_weight,
        neigh_weight,
        bias.reshape(1, W),
        out_grad,
    )
    return output, grad_features, self_grad, neigh_grad, bias_grad.reshape(W)


def solution(mesh):
    placed = (
        P(("row", "col"), None),
        P(("row", "col")),
        P("row", "col", None, None, None, None),
        P("row", "col", None, None),
        P("row", "col", None),
        P(),
        P(),
        P(),
        P(("row", "col"), None),
    )
    return jax.shard_map(
        local,
        mesh=mesh,
        in_specs=placed,
        out_specs=(P(("row", "col"), None), P(("row", "col"), None), P(), P(), P()),
        check_vma=False,
    )
```

time: 571 us -> 87.2 us (0.15)
  waiting for transfers between devices: 371 us -> 0 us
  Pallas kernels: 0 us -> 76.6 us
  blocking collectives: 75.5 us -> 0 us
  other arithmetic: 50.3 us -> 1.45 us
  matrix products: 34 us -> 0 us
  local copies, waits for them, and re-layouts: 22.4 us -> 8.22 us
  between operations: 14 us -> 0.64 us
    reduce_scatter x2 -> x0, waiting for transfers between devices: 148 us -> none  [the longest x1 86.4 us: local(): lax.psum_scatter(summed[:span_tiles].reshape(row_total, feat_width), 'col...]
    psum x1 -> x0, waiting for transfers between devices: 134 us -> none  [local(): lax.psum((self_part, neigh_part, bias_part), ('row', 'col'))]
    all_gather x2 -> x0, waiting for transfers between devices: 88.2 us -> none  [the longest x1 48.6 us: local(): lax.all_gather(scaled_grad, 'col', axis=0, tiled=True)]
    pallas_call x0 -> x1, Pallas kernels: none -> 76.6 us  [local(): pl.pallas_call(kernel, out_shape=(jax.ShapeDtypeStruct((T, W), BF16), jax...]
    psum x1 -> x0, blocking collectives: 75.5 us -> none  [local(): lax.psum((self_part, neigh_part, bias_part), ('row', 'col'))]
    scatter-add x2 -> x0, other arithmetic: 48.5 us -> none  [the longest x1 24.4 us: local(): jax.ops.segment_sum(flat_products, keys, num_segments=span_tiles + 1)]
    dot_general x8 -> x0, matrix products: 34 us -> none  [the longest x1 13.9 us: local(): jnp.einsum('pkab,pkaf->pkbf', masked, source, preferred_element_type=jnp....]
    gather x2 -> x0, local copies, waits for them, and re-layouts: 15.9 us -> none  [the longest x1 8.07 us: local(): column_feats[jnp.arange(piece_total, dtype=jnp.int32)[:, None], tile_cols]]
  transfers between devices with their start and end apart: 5 -> 0, of which waited for: 5 -> 0; matrix products, arithmetic and copies ran while one was open for 9% -> 0% of each run, Pallas kernels for 0% -> 0%
where the time goes in v1:
time: 87.2 us; the launch traced here: 86.9 us
  Pallas kernels  76.6 us (88%)
  local copies, waits for them, and re-layouts  8.22 us (9%)
  other arithmetic  1.45 us (2%)
    pallas_call x1, Pallas kernels, local(): pl.pallas_call(kernel, out_shape=(jax.ShapeDtypeStruct((T, W), BF16), jax...  76.6 us
    unnamed x5, local copies, waits for them, and re-layouts  7.46 us

profile of v1, /device:TPU:1, one launch (start us, length us, event | category | flops | bytes accessed | tf_op | source)
XLA Modules:
  0.0 86.9 jit_solution(1961293143068642001)
XLA Ops:
  0.6 0.7 iota_compare_fusion.1
  1.4 0.8 copy.15
  2.1 0.7 select_reduce_fusion.slot_s
  2.8 76.6 %sage.1 = (bf16[128,256]{1,0:T(8,128)(2,1)}, bf16[128,256]{1,0:T(8,128)(2,1)}, f32[256,256]{1,0:T(8,128)}, f32[256,256]{1,0:T(8,128)}, f32[1,256]{1,0:T(1,128)}) custom-call(s32[16,16]{1,0:T(8,128)} %select_reduce_fusion.slot_s, bf16[128,256]{1,0:T(8,128)(2,1)} %feats_h.1, s32[1,128]{1,0:T(1,128)} %bitcast.11, bf16[128,128,128]{2,1,0:T(8,128)(2,1)} %bitcast.6, ...), custom_call_target="tpu_custom_call" | custom-call | tf_op jit(solution)/shard_map/sage/pallas_call | solution.py:394
  79.4 1.5 %copy.21 = bf16[128,256]{1,0:T(8,128)(2,1)} copy(bf16[128,256]{1,0:T(8,128)(2,1)} %get-tuple-element.20) | data formatting | bytes 131072
  80.9 1.5 %copy.22 = bf16[128,256]{1,0:T(8,128)(2,1)} copy(bf16[128,256]{1,0:T(8,128)(2,1)} %get-tuple-element.21) | data formatting | bytes 131072
  82.4 1.7 %copy.23 = f32[256,256]{1,0:T(8,128)} copy(f32[256,256]{1,0:T(8,128)} %get-tuple-element.22) | data formatting | bytes 524288
  84.0 1.7 %copy.24 = f32[256,256]{1,0:T(8,128)} copy(f32[256,256]{1,0:T(8,128)} %get-tuple-element.23) | data formatting | bytes 524288
  85.7 1.2 %copy.25 = f32[256]{0:T(256)} copy(f32[256]{0:T(256)} %bitcast.8) | data formatting | bytes 2048

commit v2 on v1

v2 whole, which is shorter than its diff:
```python
import functools

import jax
import jax.numpy as jnp
from jax import lax
from jax.experimental import pallas as pl
from jax.experimental.pallas import tpu as pltpu
from jax.sharding import PartitionSpec as P

MESH = pl.DeviceIdType.MESH
F32 = jnp.float32
BF16 = jnp.bfloat16
T = 128
W = 256
CHIPS = [(dx, dz) for dx in (2, 1, 3, 0) for dz in (1, 0) if dx or dz]
PLANE = [(dx, dy) for dx in range(4) for dy in range(4) if dx or dy]
FAR = (2, 1, 3)
GELU_C = 0.7978845608028654


def dot(lhs, rhs, lhs_dim=1, rhs_dim=0):
    return lax.dot_general(
        lhs, rhs, (((lhs_dim,), (rhs_dim,)), ((), ())), preferred_element_type=F32
    )


def device(x, zl, c, y, zh):
    return (x * 4 + zl * 2 + c, y * 4 + zh)


def piece_at(x, zl, c):
    return x * 4 + c * 2 + zl


def split_rows(total):
    high = total.astype(BF16).astype(F32)
    return high, total - high


def bias_block(total):
    high, low = split_rows(total)
    line = lax.broadcasted_iota(jnp.int32, (16, W), 0)
    return jnp.where(line == 0, high, jnp.where(line == 1, low, 0.0)).astype(BF16)


def kernel(
    feats_h, deg_h, tiles_h, index_h, count_h, ws_h, wn_h, bias_h, og_h,
    out_v, gf_v, ar4, ar5_r, bg_v,
    tiles, dense, index_v, count_v, slot_v, slot_s, feats_all, grads_all,
    deg_v, ws, wn, bias_v, og_v, base, recip, part_b, recv_by, sum_z, recv_bz, self_keep,
    part_d, recv_ds, sum_d, recv_d, ar1_s, ar1_r, ar2_s, ar2_r, ar3_s, ar3_r,
    local_sem, a_ss, a_rs, af_ss, af_rs, by_ss, by_rs, bz_ss, bz_rs,
    cz_ss, cz_rs, cy_ss, cy_rs, ds_ss, ds_rs, d_ss, d_rs,
    r1_ss, r1_rs, r2_ss, r2_rs, r3_ss, r3_rs, r4_ss, r4_rs, r5_ss, r5_rs,
):
    a = lax.axis_index("row")
    b = lax.axis_index("col")
    x, zl, c = a // 4, (a // 2) % 2, a % 2
    y, zh = b // 4, b % 4
    z = zh * 2 + zl
    sib = device(x, zl, 1 - c, y, zh)
    home = piece_at(x, zl, c)
    sent = []

    def send(src, dst, send_sem, recv_sem, where):
        copy = pltpu.make_async_remote_copy(
            src_ref=src, dst_ref=dst, send_sem=send_sem, recv_sem=recv_sem,
            device_id=where, device_id_type=MESH,
        )
        copy.start()
        sent.append(copy)
        return copy

    def chip(dx, dz):
        return (x + dx) % 4, (zl + dz) % 2

    loads = [
        pltpu.make_async_copy(
            feats_h.at[:, pl.ds(h * T, T)], feats_all.at[h, home], local_sem.at[h]
        )
        for h in range(2)
    ]
    small = [
        pltpu.make_async_copy(index_h, index_v, local_sem.at[2]),
        pltpu.make_async_copy(count_h, count_v, local_sem.at[3]),
    ]
    large = [
        pltpu.make_async_copy(ws_h, ws, local_sem.at[4]),
        pltpu.make_async_copy(wn_h, wn, local_sem.at[5]),
        pltpu.make_async_copy(bias_h, bias_v, local_sem.at[6]),
        pltpu.make_async_copy(og_h, og_v, local_sem.at[7]),
        pltpu.make_async_copy(deg_h, deg_v, local_sem.at[8]),
        pltpu.make_async_copy(tiles_h, tiles, local_sem.at[9]),
    ]
    for load in loads + small + large:
        load.start()

    partners = [sib]
    partners += [device(*chip(dx, dz), c, y, zh) for dx, dz in CHIPS]
    partners += [device((x + dx) % 4, zl, c, (y + dy) % 4, zh) for dx, dy in PLANE if dy]
    partners += [
        device(x, zz % 2, c, y, zz // 2)
        for zz in [(z + d) % 8 for d in range(1, 8)]
    ]
    barrier = pltpu.get_barrier_semaphore()
    for partner in partners:
        pl.semaphore_signal(barrier, inc=1, device_id=partner, device_id_type=MESH)

    for load in small:
        load.wait()
    place = lax.broadcasted_iota(jnp.int32, (16, 16), 0)
    slot = jnp.full((16, 16), 8, jnp.int32)
    for k in range(8):
        here = (index_v[k : k + 1] == place) & (count_v[...] > k)
        slot = jnp.where(here, k, slot)
    slot_v[:, 0:16] = slot
    to_scalar = pltpu.make_async_copy(slot_v, slot_s, local_sem.at[10])
    to_scalar.start()
    for load in loads:
        load.wait()
    pl.semaphore_wait(barrier, len(partners))

    a_sent = []
    for h in range(2):
        mine = feats_all.at[h, home]
        a_sent.append(
            [
                send(mine, mine, a_ss.at[h, j], a_rs.at[h, j], device(*chip(dx, dz), c, y, zh))
                for j, (dx, dz) in enumerate(CHIPS)
            ]
            + [send(mine, mine, a_ss.at[h, 7], a_rs.at[h, 7], sib)]
        )

    to_scalar.wait()
    for load in large:
        load.wait()

    def build(q, carry):
        r = (q % 4) * 4 + q // 4
        for p in range(16):
            at = piece_at(p // 4, (p // 2) % 2, p % 2)
            slot = slot_s[r, p]
            tile = tiles[p * 8 + jnp.minimum(slot, 7)]
            dense[q, :, at * T : (at + 1) * T] = jnp.where(
                slot < 8, tile, jnp.zeros_like(tile)
            )
        return carry

    lax.fori_loop(0, 16, build, 0)
    feats = jnp.concatenate([feats_all[0, home], feats_all[1, home]], axis=1)
    base[...] = dot(feats, ws[...]) + bias_v[...]
    inverse = jnp.broadcast_to(1.0 / deg_v[...].astype(F32), (T, T)).T
    recip[...] = inverse

    by_sent = []
    for h in range(2):
        forwards = []
        for j in (4, 1, 3, 5, 6, 0, 2):
            dx, dz = CHIPS[j]
            a_sent[h][j].wait_recv()
            piece = feats_all.at[h, piece_at(*chip(-dx, dz), c)]
            forwards.append(send(piece, piece, af_ss.at[h, j], af_rs.at[h, j], sib))
        a_sent[h][7].wait_recv()
        for copy in forwards:
            copy.wait_recv()
        gathered = feats_all[h].reshape(16 * T, T)
        for i, dz in enumerate((2, 1, 3, 0)):
            zz = (zh + dz) % 4
            part = dot(dense[pl.ds(zz * 4, 4)].reshape(4 * T, 16 * T), gathered)
            part_b[h, i] = part.reshape(4, T, T).astype(BF16)
            row = []
            for k, dy in enumerate(FAR):
                yy = (y + dy) % 4
                row.append(
                    send(
                        part_b.at[h, i, yy], recv_by.at[h, i, k],
                        by_ss.at[h, i, k], by_rs.at[h, i, k], device(x, zl, c, yy, zh),
                    )
                )
            by_sent.append(row)

    bz_sent = []
    owns = []
    for h in range(2):
        for i, dz in enumerate((2, 1, 3, 0)):
            total = part_b[h, i, y].astype(F32)
            for k in range(3):
                by_sent[h * 4 + i][k].wait_recv()
                total = total + recv_by[h, i, k].astype(F32)
            if dz:
                sum_z[h, i] = total.astype(BF16)
                bz_sent.append(
                    send(
                        sum_z.at[h, i], recv_bz.at[h, i], bz_ss.at[h, i], bz_rs.at[h, i],
                        device(x, zl, c, y, (zh + dz) % 4),
                    )
                )
            else:
                owns.append(total)
    means = []
    pre = base[...]
    for h in range(2):
        total = owns[h]
        for i in range(3):
            bz_sent[h * 3 + i].wait_recv()
            total = total + recv_bz[h, i].astype(F32)
        means.append((total * recip[...]).astype(BF16))
        pre = pre + dot(means[h], wn[h * T : (h + 1) * T])

    tanh = jnp.tanh(GELU_C * (pre + 0.044715 * (pre * pre * pre)))
    slope = 0.5 * (1.0 + tanh) + 0.5 * pre * (1.0 - tanh * tanh) * (
        GELU_C * (1.0 + 3.0 * 0.044715 * (pre * pre))
    )
    gp = (og_v[...].astype(F32) * slope).astype(BF16)

    me = zh * 4 + y
    cz_sent = []
    cy_sent = [[], []]
    for h in range(2):
        mine = grads_all.at[h, me]
        grads_all[h, me] = (dot(gp, wn[h * T : (h + 1) * T], 1, 1) * recip[...]).astype(BF16)
        cz_sent.append(
            [
                send(
                    mine, mine, cz_ss.at[h, k], cz_rs.at[h, k],
                    device(x, zl, c, y, (zh + d) % 4),
                )
                for k, d in enumerate(FAR)
            ]
        )
        for k, d in enumerate(FAR):
            cy_sent[h].append(
                send(
                    mine, mine, cy_ss.at[h, 3, k], cy_rs.at[h, 3, k],
                    device(x, zl, c, (y + d) % 4, zh),
                )
            )

    out_v[...] = (0.5 * pre * (1.0 + tanh)).astype(BF16)

    mean = jnp.concatenate(means, axis=1)
    feats = jnp.concatenate([feats_all[0, home], feats_all[1, home]], axis=1)
    self_part = dot(feats, gp, 0, 0)
    neigh_part = dot(mean, gp, 0, 0)
    bias_part = jnp.sum(gp.astype(F32), axis=0, keepdims=True)
    first = c == 0
    ar1_s[0:W] = jnp.where(first, neigh_part, self_part).astype(BF16)
    ar1_s[W : W + 16] = bias_block(bias_part)
    r1 = send(ar1_s, ar1_r, r1_ss, r1_rs, sib)
    keep = jnp.where(first, self_part, neigh_part)
    self_keep[...] = dot(gp, ws[...], 1, 1)
    r1.wait_recv()
    chunk = keep + ar1_r[0:W].astype(F32)
    ar2_s[:, 0:16] = chunk.reshape(16, 16, W).astype(BF16)
    other = ar1_r[W : W + 16].astype(F32)
    mine = ar1_s[W : W + 16].astype(F32)
    both = jnp.sum(mine + other, axis=0, keepdims=True)
    ar2_s[:, 16:32] = jnp.broadcast_to(bias_block(both)[None], (16, 16, W))
    spot = x * 4 + y
    r2 = []
    for j, (dx, dy) in enumerate(PLANE):
        xx, yy = (x + dx) % 4, (y + dy) % 4
        r2.append(
            send(
                ar2_s.at[xx * 4 + yy], ar2_r.at[spot], r2_ss.at[j], r2_rs.at[j],
                device(xx, zl, c, yy, zh),
            )
        )
    ar2_r[spot] = ar2_s[spot]

    for h in range(2):
        for k in (1, 2, 0):
            cz_sent[h][k].wait_recv()
            piece = grads_all.at[h, ((zh - FAR[k]) % 4) * 4 + y]
            for m, dy in enumerate(FAR):
                cy_sent[h].append(
                    send(
                        piece, piece, cy_ss.at[h, k, m], cy_rs.at[h, k, m],
                        device(x, zl, c, (y + dy) % 4, zh),
                    )
                )

    for copy in r2:
        copy.wait_recv()
    total = jnp.zeros((32, W), F32)
    for j in range(16):
        total = total + ar2_r[j].astype(F32)
    ar3_s[0:16] = total[0:16].astype(BF16)
    ar3_s[16:32] = bias_block(jnp.sum(total[16:32], axis=0, keepdims=True))
    r3 = []
    for j in range(7):
        zz = (z + j + 1) % 8
        r3.append(
            send(
                ar3_s, ar3_r.at[z], r3_ss.at[j], r3_rs.at[j], device(x, zz % 2, c, y, zz // 2)
            )
        )
    ar3_r[z] = ar3_s[...]

    ds_sent = []
    d_sent = [[], []]

    def terms(h, i):
        xx = (x + (2, 1, 3, 0)[i]) % 4
        columns = pl.ds(pl.multiple_of(xx * 4 * T, 4 * T), 4 * T)
        block = dense[:, :, columns].reshape(16 * T, 4 * T)
        part = dot(block, grads_all[h].reshape(16 * T, T), 0, 0)
        part_d[h, i] = part.reshape(2, 2, T, T).astype(BF16)
        ds_sent.append(
            send(part_d.at[h, i, 1 - c], recv_ds.at[h, i], ds_ss.at[h, i], ds_rs.at[h, i], sib)
        )

    def pass_on(h, i):
        dx = (2, 1, 3, 0)[i]
        ds_sent[h * 4 + i].wait_recv()
        total = part_d[h, i, c].astype(F32) + recv_ds[h, i].astype(F32)
        sum_d[h, i] = total.astype(BF16)
        for dz in (1, 0):
            if dx or dz:
                xx, zz = chip(dx, dz)
                j = CHIPS.index((dx, dz))
                d_sent[h].append(
                    send(
                        sum_d.at[h, i, zz], recv_d.at[h, j], d_ss.at[h, j], d_rs.at[h, j],
                        device(xx, zz, c, y, zh),
                    )
                )

    for copy in cy_sent[0]:
        copy.wait_recv()
    for i in range(4):
        terms(0, i)
        if i:
            pass_on(0, i - 1)
    pass_on(0, 3)

    for copy in r3:
        copy.wait_recv()
    total = jnp.zeros((32, W), F32)
    for j in range(8):
        total = total + ar3_r[j].astype(F32)
    bg_v[...] = jnp.sum(total[16:32], axis=0, keepdims=True)
    ar4[spot] = total[0:16].astype(BF16)
    r4 = []
    for j, (dx, dy) in enumerate(PLANE):
        xx, yy = (x + dx) % 4, (y + dy) % 4
        r4.append(
            send(
                ar4.at[spot], ar4.at[spot], r4_ss.at[j], r4_rs.at[j], device(xx, zl, c, yy, zh)
            )
        )

    for copy in cy_sent[1]:
        copy.wait_recv()
    for i in range(4):
        terms(1, i)
        if i:
            pass_on(1, i - 1)
    pass_on(1, 3)

    for copy in r4:
        copy.wait_recv()
    r5 = send(ar4, ar5_r, r5_ss, r5_rs, sib)

    for h in range(2):
        back = self_keep[:, h * T : (h + 1) * T] + sum_d[h, 3, zl].astype(F32)
        for copy in d_sent[h]:
            copy.wait_recv()
        for j in range(7):
            back = back + recv_d[h, j].astype(F32)
        gf_v[:, h * T : (h + 1) * T] = back.astype(BF16)
    r5.wait_recv()
    for copy in sent:
        copy.wait_send()


def finish(out_v, gf_v, ar4, ar5_r, bg_v, out_h, gf_h, sg_h, ng_h, bg_h, sg_v, ng_v, sem):
    stores = [
        pltpu.make_async_copy(out_v, out_h, sem.at[0]),
        pltpu.make_async_copy(gf_v, gf_h, sem.at[1]),
        pltpu.make_async_copy(bg_v, bg_h, sem.at[2]),
        pltpu.make_async_copy(sg_v, sg_h, sem.at[3]),
        pltpu.make_async_copy(ng_v, ng_h, sem.at[4]),
    ]
    for store in stores[:3]:
        store.start()
    first = lax.axis_index("row") % 2 == 0
    here = ar4[...].reshape(W, W).astype(F32)
    there = ar5_r[...].reshape(W, W).astype(F32)
    sg_v[...] = jnp.where(first, here, there)
    stores[3].start()
    ng_v[...] = jnp.where(first, there, here)
    stores[4].start()
    for store in stores:
        store.wait()


def local(
    features, degrees, tile_values, tile_index, tile_count, self_weight, neigh_weight, bias,
    out_grad,
):
    vm = pltpu.VMEM
    dma = pltpu.SemaphoreType.DMA
    anywhere = pl.BlockSpec(memory_space=pl.ANY)
    inside = pl.BlockSpec(memory_space=pltpu.VMEM)
    scratch = [
        vm((128, T, T), BF16), vm((16, T, 16 * T), BF16),
        vm((8, 16), jnp.int32), vm((1, 16), jnp.int32), vm((16, T), jnp.int32),
        pltpu.SMEM((16, T), jnp.int32),
        vm((2, 16, T, T), BF16), vm((2, 16, T, T), BF16),
        vm((1, T), jnp.int32), vm((W, W), BF16), vm((W, W), BF16), vm((1, W), F32),
        vm((T, W), BF16),
        vm((T, W), F32), vm((T, T), F32),
        vm((2, 4, 4, T, T), BF16), vm((2, 4, 3, T, T), BF16), vm((2, 3, T, T), BF16),
        vm((2, 3, T, T), BF16), vm((T, W), F32),
        vm((2, 4, 2, 2, T, T), BF16), vm((2, 4, 2, T, T), BF16), vm((2, 4, 2, T, T), BF16),
        vm((2, 7, T, T), BF16),
        vm((W + 16, W), BF16), vm((W + 16, W), BF16),
        vm((16, 32, W), BF16), vm((16, 32, W), BF16),
        vm((32, W), BF16), vm((8, 32, W), BF16),
        dma((11,)), dma((2, 8)), dma((2, 8)), dma((2, 7)), dma((2, 7)),
        dma((2, 4, 3)), dma((2, 4, 3)), dma((2, 3)), dma((2, 3)),
        dma((2, 3)), dma((2, 3)), dma((2, 4, 3)), dma((2, 4, 3)),
        dma((2, 4)), dma((2, 4)), dma((2, 7)), dma((2, 7)),
        dma(()), dma(()), dma((15,)), dma((15,)), dma((7,)), dma((7,)),
        dma((15,)), dma((15,)), dma(()), dma(()),
    ]
    raw = pl.pallas_call(
        kernel,
        out_shape=(
            jax.ShapeDtypeStruct((T, W), BF16),
            jax.ShapeDtypeStruct((T, W), BF16),
            jax.ShapeDtypeStruct((16, 16, W), BF16),
            jax.ShapeDtypeStruct((16, 16, W), BF16),
            jax.ShapeDtypeStruct((1, W), F32),
        ),
        in_specs=[anywhere] * 9,
        out_specs=[inside] * 5,
        scratch_shapes=scratch,
        compiler_params=pltpu.CompilerParams(
            collective_id=0, has_side_effects=True, vmem_limit_bytes=58 * 2**20
        ),
        name="sage",
    )(
        features,
        degrees.reshape(1, T),
        tile_values.reshape(128, T, T),
        tile_index.reshape(16, 8).T,
        tile_count.reshape(1, 16),
        self_weight,
        neigh_weight,
        bias.reshape(1, W),
        out_grad,
    )
    output, grad_features, self_grad, neigh_grad, bias_grad = pl.pallas_call(
        finish,
        out_shape=(
            jax.ShapeDtypeStruct((T, W), BF16),
            jax.ShapeDtypeStruct((T, W), BF16),
            jax.ShapeDtypeStruct((W, W), F32),
            jax.ShapeDtypeStruct((W, W), F32),
            jax.ShapeDtypeStruct((1, W), F32),
        ),
        in_specs=[inside] * 5,
        out_specs=[anywhere] * 5,
        scratch_shapes=[vm((W, W), F32), vm((W, W), F32), dma((5,))],
        compiler_params=pltpu.CompilerParams(vmem_limit_bytes=62 * 2**20),
        name="finish",
    )(*raw)
    return output, grad_features, self_grad, neigh_grad, bias_grad.reshape(W)


def solution(mesh):
    placed = (
        P(("row", "col"), None),
        P(("row", "col")),
        P("row", "col", None, None, None, None),
        P("row", "col", None, None),
        P("row", "col", None),
        P(),
        P(),
        P(),
        P(("row", "col"), None),
    )
    return jax.shard_map(
        local,
        mesh=mesh,
        in_specs=placed,
        out_specs=(P(("row", "col"), None), P(("row", "col"), None), P(), P(), P()),
        check_vma=False,
    )
```

time: 87.2 us -> 71.6 us (0.82)
  local copies, waits for them, and re-layouts: 8.22 us -> 0 us
  Pallas kernels: 76.6 us -> 70.8 us
  other arithmetic: 1.45 us -> 0 us
    pallas_call x1, Pallas kernels: 76.6 us -> 68.9 us  [local(): pl.pallas_call(kernel, out_shape=(jax.ShapeDtypeStruct((T, W), BF16), jax...]
    unnamed x5 -> x0, local copies, waits for them, and re-layouts: 7.46 us -> none
    pallas_call x0 -> x1, Pallas kernels: none -> 1.92 us  [local(): pl.pallas_call(finish, out_shape=(jax.ShapeDtypeStruct((T, W), BF16), jax...]
where the time goes in v2:
time: 71.6 us; the launch traced here: 71.5 us
  Pallas kernels  70.8 us (99%)
    pallas_call x1, Pallas kernels, local(): pl.pallas_call(kernel, out_shape=(jax.ShapeDtypeStruct((T, W), BF16), jax...  68.9 us
    pallas_call x1, Pallas kernels, local(): pl.pallas_call(finish, out_shape=(jax.ShapeDtypeStruct((T, W), BF16), jax...  1.92 us

profile of v2, /device:TPU:1, one launch (start us, length us, event | category | flops | bytes accessed | tf_op | source)
XLA Modules:
  0.0 71.5 jit_solution(12373626423756986063)
XLA Ops:
  0.6 68.9 %sage.1 = (bf16[128,256]{1,0:T(8,128)(2,1)}, bf16[128,256]{1,0:T(8,128)(2,1)}, bf16[16,16,256]{2,1,0:T(8,128)(2,1)}, bf16[16,16,256]{2,1,0:T(8,128)(2,1)}, f32[1,256]{1,0:T(1,128)}) custom-call(bf16[128,256]{1,0:T(8,128)(2,1)} %feats_h.1, s32[1,128]{1,0:T(1,128)} %bitcast.11, bf16[128,128,128]{2,1,0:T(8,128)(2,1)} %bitcast.8, s32[8,16]{1,0:T(8,128)} %bitcast.9, ...), custom_call_target="tpu_custom_call" | custom-call | tf_op jit(solution)/shard_map/sage/pallas_call | solution.py:428
  69.5 1.9 %finish.1 = (bf16[128,256]{1,0:T(8,128)(2,1)}, bf16[128,256]{1,0:T(8,128)(2,1)}, f32[256,256]{1,0:T(8,128)}, f32[256,256]{1,0:T(8,128)}, f32[1,256]{1,0:T(1,128)}) custom-call(bf16[128,256]{1,0:T(8,128)(2,1)} %get-tuple-element.15.out_v, bf16[128,256]{1,0:T(8,128)(2,1)} %get-tuple-element.16.gf_v, bf16[16,16,256]{2,1,0:T(8,128)(2,1)} %get-tuple-element.17.ar4, ...), custom_call_target="tpu_custom_call" | custom-call | tf_op jit(solution)/shard_map/finish/pallas_call | solution.py:455

commit v3 on v2

--- a/solution.py
+++ b/solution.py
@@ -15,6 +15,7 @@
 CHIPS = [(dx, dz) for dx in (2, 1, 3, 0) for dz in (1, 0) if dx or dz]
 PLANE = [(dx, dy) for dx in range(4) for dy in range(4) if dx or dy]
 FAR = (2, 1, 3)
+FAR_FIRST = (2, 1, 3, 0)
 GELU_C = 0.7978845608028654
 
 
@@ -29,7 +30,7 @@
 
 
 def piece_at(x, zl, c):
-    return x * 4 + c * 2 + zl
+    return c * 8 + x * 2 + zl
 
 
 def split_rows(total):
@@ -47,8 +48,8 @@
     feats_h, deg_h, tiles_h, index_h, count_h, ws_h, wn_h, bias_h, og_h,
     out_v, gf_v, ar4, ar5_r, bg_v,
     tiles, dense, index_v, count_v, slot_v, slot_s, feats_all, grads_all,
-    deg_v, ws, wn, bias_v, og_v, base, recip, part_b, recv_by, sum_z, recv_bz, self_keep,
-    part_d, recv_ds, sum_d, recv_d, ar1_s, ar1_r, ar2_s, ar2_r, ar3_s, ar3_r,
+    deg_v, ws, wn, bias_v, og_v, base, recip, sums, part_b, recv_by, sum_z, recv_bz, self_keep,
+    part_d, keep_d, recv_ds, sum_d, recv_d, ar1_s, ar1_r, ar2_s, ar2_r, ar3_s, ar3_r,
     local_sem, a_ss, a_rs, af_ss, af_rs, by_ss, by_rs, bz_ss, bz_rs,
     cz_ss, cz_rs, cy_ss, cy_rs, ds_ss, ds_rs, d_ss, d_rs,
     r1_ss, r1_rs, r2_ss, r2_rs, r3_ss, r3_rs, r4_ss, r4_rs, r5_ss, r5_rs,
@@ -74,27 +75,6 @@
     def chip(dx, dz):
         return (x + dx) % 4, (zl + dz) % 2
 
-    loads = [
-        pltpu.make_async_copy(
-            feats_h.at[:, pl.ds(h * T, T)], feats_all.at[h, home], local_sem.at[h]
-        )
-        for h in range(2)
-    ]
-    small = [
-        pltpu.make_async_copy(index_h, index_v, local_sem.at[2]),
-        pltpu.make_async_copy(count_h, count_v, local_sem.at[3]),
-    ]
-    large = [
-        pltpu.make_async_copy(ws_h, ws, local_sem.at[4]),
-        pltpu.make_async_copy(wn_h, wn, local_sem.at[5]),
-        pltpu.make_async_copy(bias_h, bias_v, local_sem.at[6]),
-        pltpu.make_async_copy(og_h, og_v, local_sem.at[7]),
-        pltpu.make_async_copy(deg_h, deg_v, local_sem.at[8]),
-        pltpu.make_async_copy(tiles_h, tiles, local_sem.at[9]),
-    ]
-    for load in loads + small + large:
-        load.start()
-
     partners = [sib]
     partners += [device(*chip(dx, dz), c, y, zh) for dx, dz in CHIPS]
     partners += [device((x + dx) % 4, zl, c, (y + dy) % 4, zh) for dx, dy in PLANE if dy]
@@ -106,6 +86,41 @@
     for partner in partners:
         pl.semaphore_signal(barrier, inc=1, device_id=partner, device_id_type=MESH)
 
+    halves = [feats_h.at[:, pl.ds(h * T, T)] for h in range(2)]
+    small = [
+        pltpu.make_async_copy(index_h, index_v, local_sem.at[2]),
+        pltpu.make_async_copy(count_h, count_v, local_sem.at[3]),
+    ]
+    large = [
+        pltpu.make_async_copy(tiles_h, tiles, local_sem.at[9]),
+        pltpu.make_async_copy(ws_h, ws, local_sem.at[4]),
+        pltpu.make_async_copy(wn_h, wn, local_sem.at[5]),
+        pltpu.make_async_copy(bias_h, bias_v, local_sem.at[6]),
+        pltpu.make_async_copy(og_h, og_v, local_sem.at[7]),
+        pltpu.make_async_copy(deg_h, deg_v, local_sem.at[8]),
+    ]
+    large += [
+        pltpu.make_async_copy(halves[h], feats_all.at[h, home], local_sem.at[h])
+        for h in range(2)
+    ]
+    for load in small + large:
+        load.start()
+    pl.semaphore_wait(barrier, len(partners))
+
+    a_sent = []
+    for h in range(2):
+        there = feats_all.at[h, home]
+        a_sent.append(
+            [
+                send(
+                    halves[h], there, a_ss.at[h, j], a_rs.at[h, j],
+                    device(*chip(dx, dz), c, y, zh),
+                )
+                for j, (dx, dz) in enumerate(CHIPS)
+            ]
+            + [send(halves[h], there, a_ss.at[h, 7], a_rs.at[h, 7], sib)]
+        )
+
     for load in small:
         load.wait()
     place = lax.broadcasted_iota(jnp.int32, (16, 16), 0)
@@ -116,21 +131,6 @@
     slot_v[:, 0:16] = slot
     to_scalar = pltpu.make_async_copy(slot_v, slot_s, local_sem.at[10])
     to_scalar.start()
-    for load in loads:
-        load.wait()
-    pl.semaphore_wait(barrier, len(partners))
-
-    a_sent = []
-    for h in range(2):
-        mine = feats_all.at[h, home]
-        a_sent.append(
-            [
-                send(mine, mine, a_ss.at[h, j], a_rs.at[h, j], device(*chip(dx, dz), c, y, zh))
-                for j, (dx, dz) in enumerate(CHIPS)
-            ]
-            + [send(mine, mine, a_ss.at[h, 7], a_rs.at[h, 7], sib)]
-        )
-
     to_scalar.wait()
     for load in large:
         load.wait()
@@ -153,6 +153,13 @@
     recip[...] = inverse
 
     by_sent = []
+
+    def shares(h, core, i):
+        zz = (zh + FAR_FIRST[i]) % 4
+        columns = pl.ds(pl.multiple_of(core * 8 * T, 8 * T), 8 * T)
+        block = dense[pl.ds(zz * 4, 4), :, columns].reshape(4 * T, 8 * T)
+        return dot(block, feats_all[h, pl.ds(core * 8, 8)].reshape(8 * T, T))
+
     for h in range(2):
         forwards = []
         for j in (4, 1, 3, 5, 6, 0, 2):
@@ -160,13 +167,14 @@
             a_sent[h][j].wait_recv()
             piece = feats_all.at[h, piece_at(*chip(-dx, dz), c)]
             forwards.append(send(piece, piece, af_ss.at[h, j], af_rs.at[h, j], sib))
+        for i in range(4):
+            sums[i] = shares(h, c, i)
         a_sent[h][7].wait_recv()
         for copy in forwards:
             copy.wait_recv()
-        gathered = feats_all[h].reshape(16 * T, T)
-        for i, dz in enumerate((2, 1, 3, 0)):
+        for i, dz in enumerate(FAR_FIRST):
             zz = (zh + dz) % 4
-            part = dot(dense[pl.ds(zz * 4, 4)].reshape(4 * T, 16 * T), gathered)
+            part = sums[i] + shares(h, 1 - c, i)
             part_b[h, i] = part.reshape(4, T, T).astype(BF16)
             row = []
             for k, dy in enumerate(FAR):
@@ -182,7 +190,7 @@
     bz_sent = []
     owns = []
     for h in range(2):
-        for i, dz in enumerate((2, 1, 3, 0)):
+        for i, dz in enumerate(FAR_FIRST):
             total = part_b[h, i, y].astype(F32)
             for k in range(3):
                 by_sent[h * 4 + i][k].wait_recv()
@@ -300,20 +308,23 @@
     ds_sent = []
     d_sent = [[], []]
 
+    def half_terms(h, core, i):
+        at = core * 8 + (x + FAR_FIRST[i]) % 4 * 2
+        columns = pl.ds(pl.multiple_of(at * T, 2 * T), 2 * T)
+        block = dense[:, :, columns].reshape(16 * T, 2 * T)
+        return dot(block, grads_all[h].reshape(16 * T, T), 0, 0).reshape(2, T, T)
+
     def terms(h, i):
-        xx = (x + (2, 1, 3, 0)[i]) % 4
-        columns = pl.ds(pl.multiple_of(xx * 4 * T, 4 * T), 4 * T)
-        block = dense[:, :, columns].reshape(16 * T, 4 * T)
-        part = dot(block, grads_all[h].reshape(16 * T, T), 0, 0)
-        part_d[h, i] = part.reshape(2, 2, T, T).astype(BF16)
+        part_d[h, i] = half_terms(h, 1 - c, i).astype(BF16)
         ds_sent.append(
-            send(part_d.at[h, i, 1 - c], recv_ds.at[h, i], ds_ss.at[h, i], ds_rs.at[h, i], sib)
-        )
+            send(part_d.at[h, i], recv_ds.at[h, i], ds_ss.at[h, i], ds_rs.at[h, i], sib)
+        )
+        keep_d[h, i] = half_terms(h, c, i)
 
     def pass_on(h, i):
-        dx = (2, 1, 3, 0)[i]
+        dx = FAR_FIRST[i]
         ds_sent[h * 4 + i].wait_recv()
-        total = part_d[h, i, c].astype(F32) + recv_ds[h, i].astype(F32)
+        total = keep_d[h, i] + recv_ds[h, i].astype(F32)
         sum_d[h, i] = total.astype(BF16)
         for dz in (1, 0):
             if dx or dz:
@@ -411,9 +422,10 @@
         vm((1, T), jnp.int32), vm((W, W), BF16), vm((W, W), BF16), vm((1, W), F32),
         vm((T, W), BF16),
         vm((T, W), F32), vm((T, T), F32),
+        vm((4, 4 * T, T), F32),
         vm((2, 4, 4, T, T), BF16), vm((2, 4, 3, T, T), BF16), vm((2, 3, T, T), BF16),
         vm((2, 3, T, T), BF16), vm((T, W), F32),
-        vm((2, 4, 2, 2, T, T), BF16), vm((2, 4, 2, T, T), BF16), vm((2, 4, 2, T, T), BF16),
+        vm((2, 4, 2, T, T), BF16), vm((2, 4, 2, T, T), F32), vm((2, 4, 2, T, T), BF16), vm((2, 4, 2, T, T), BF16),
         vm((2, 7, T, T), BF16),
         vm((W + 16, W), BF16), vm((W + 16, W), BF16),
         vm((16, 32, W), BF16), vm((16, 32, W), BF16),

time: 71.6 us -> 67.8 us (0.947)
  Pallas kernels: 70.8 us -> 67 us
    pallas_call x1, Pallas kernels: 68.9 us -> 65.1 us  [local(): pl.pallas_call(kernel, out_shape=(jax.ShapeDtypeStruct((T, W), BF16), jax...]
where the time goes in v3:
time: 67.8 us; the launch traced here: 67.7 us
  Pallas kernels  67 us (99%)
    pallas_call x1, Pallas kernels, local(): pl.pallas_call(kernel, out_shape=(jax.ShapeDtypeStruct((T, W), BF16), jax...  65.1 us
    pallas_call x1, Pallas kernels, local(): pl.pallas_call(finish, out_shape=(jax.ShapeDtypeStruct((T, W), BF16), jax...  1.92 us

profile of v3, /device:TPU:1, one launch (start us, length us, event | category | flops | bytes accessed | tf_op | source)
XLA Modules:
  0.0 67.7 jit_solution(7941361582276389120)
XLA Ops:
  0.6 65.1 %sage.1 = (bf16[128,256]{1,0:T(8,128)(2,1)}, bf16[128,256]{1,0:T(8,128)(2,1)}, bf16[16,16,256]{2,1,0:T(8,128)(2,1)}, bf16[16,16,256]{2,1,0:T(8,128)(2,1)}, f32[1,256]{1,0:T(1,128)}) custom-call(bf16[128,256]{1,0:T(8,128)(2,1)} %feats_h.1, s32[1,128]{1,0:T(1,128)} %bitcast.11, bf16[128,128,128]{2,1,0:T(8,128)(2,1)} %bitcast.8, s32[8,16]{1,0:T(8,128)} %bitcast.9, ...), custom_call_target="tpu_custom_call" | custom-call | tf_op jit(solution)/shard_map/sage/pallas_call | solution.py:440
  65.7 1.9 %finish.1 = (bf16[128,256]{1,0:T(8,128)(2,1)}, bf16[128,256]{1,0:T(8,128)(2,1)}, f32[256,256]{1,0:T(8,128)}, f32[256,256]{1,0:T(8,128)}, f32[1,256]{1,0:T(1,128)}) custom-call(bf16[128,256]{1,0:T(8,128)(2,1)} %get-tuple-element.15.out_v, bf16[128,256]{1,0:T(8,128)(2,1)} %get-tuple-element.16.gf_v, bf16[16,16,256]{2,1,0:T(8,128)(2,1)} %get-tuple-element.17.ar4, ...), custom_call_target="tpu_custom_call" | custom-call | tf_op jit(solution)/shard_map/finish/pallas_call | solution.py:467

commit v4 on v3

--- a/solution.py
+++ b/solution.py
@@ -46,8 +46,8 @@
 
 def kernel(
     feats_h, deg_h, tiles_h, index_h, count_h, ws_h, wn_h, bias_h, og_h,
-    out_v, gf_v, ar4, ar5_r, bg_v,
-    tiles, dense, index_v, count_v, slot_v, slot_s, feats_all, grads_all,
+    out_h, gf_h, sg_h, ng_h, bg_h,
+    out_v, gf_v, ar4, ar5_r, sg_v, ng_v, bg_v, tiles, dense, index_v, count_v, slot_v, slot_s, feats_all, grads_all,
     deg_v, ws, wn, bias_v, og_v, base, recip, sums, part_b, recv_by, sum_z, recv_bz, self_keep,
     part_d, keep_d, recv_ds, sum_d, recv_d, ar1_s, ar1_r, ar2_s, ar2_r, ar3_s, ar3_r,
     local_sem, a_ss, a_rs, af_ss, af_rs, by_ss, by_rs, bz_ss, bz_rs,
@@ -108,7 +108,8 @@
     pl.semaphore_wait(barrier, len(partners))
 
     a_sent = []
-    for h in range(2):
+
+    def send_half(h):
         there = feats_all.at[h, home]
         a_sent.append(
             [
@@ -120,6 +121,8 @@
             ]
             + [send(halves[h], there, a_ss.at[h, 7], a_rs.at[h, 7], sib)]
         )
+
+    send_half(0)
 
     for load in small:
         load.wait()
@@ -147,6 +150,7 @@
         return carry
 
     lax.fori_loop(0, 16, build, 0)
+    send_half(1)
     feats = jnp.concatenate([feats_all[0, home], feats_all[1, home]], axis=1)
     base[...] = dot(feats, ws[...]) + bias_v[...]
     inverse = jnp.broadcast_to(1.0 / deg_v[...].astype(F32), (T, T)).T
@@ -245,6 +249,8 @@
             )
 
     out_v[...] = (0.5 * pre * (1.0 + tanh)).astype(BF16)
+    stores = [pltpu.make_async_copy(out_v, out_h, local_sem.at[11])]
+    stores[0].start()
 
     mean = jnp.concatenate(means, axis=1)
     feats = jnp.concatenate([feats_all[0, home], feats_all[1, home]], axis=1)
@@ -373,35 +379,42 @@
         copy.wait_recv()
     r5 = send(ar4, ar5_r, r5_ss, r5_rs, sib)
 
-    for h in range(2):
+    def total_back(h):
         back = self_keep[:, h * T : (h + 1) * T] + sum_d[h, 3, zl].astype(F32)
         for copy in d_sent[h]:
             copy.wait_recv()
         for j in range(7):
             back = back + recv_d[h, j].astype(F32)
         gf_v[:, h * T : (h + 1) * T] = back.astype(BF16)
+
+    total_back(0)
     r5.wait_recv()
-    for copy in sent:
-        copy.wait_send()
-
-
-def finish(out_v, gf_v, ar4, ar5_r, bg_v, out_h, gf_h, sg_h, ng_h, bg_h, sg_v, ng_v, sem):
-    stores = [
-        pltpu.make_async_copy(out_v, out_h, sem.at[0]),
-        pltpu.make_async_copy(gf_v, gf_h, sem.at[1]),
-        pltpu.make_async_copy(bg_v, bg_h, sem.at[2]),
-        pltpu.make_async_copy(sg_v, sg_h, sem.at[3]),
-        pltpu.make_async_copy(ng_v, ng_h, sem.at[4]),
-    ]
-    for store in stores[:3]:
-        store.start()
-    first = lax.axis_index("row") % 2 == 0
     here = ar4[...].reshape(W, W).astype(F32)
     there = ar5_r[...].reshape(W, W).astype(F32)
     sg_v[...] = jnp.where(first, here, there)
-    stores[3].start()
     ng_v[...] = jnp.where(first, there, here)
-    stores[4].start()
+    stores += [
+        pltpu.make_async_copy(sg_v, sg_h, local_sem.at[12]),
+        pltpu.make_async_copy(ng_v, ng_h, local_sem.at[13]),
+        pltpu.make_async_copy(bg_v, bg_h, local_sem.at[14]),
+    ]
+    for store in stores[1:]:
+        store.start()
+    for copy in sent:
+        copy.wait_send()
+    total_back(1)
+    stores.append(pltpu.make_async_copy(gf_v, gf_h, local_sem.at[15]))
+    stores[-1].start()
+    for store in stores:
+        store.wait()
+
+
+def finish(*refs):
+    stores = [
+        pltpu.make_async_copy(refs[i], refs[5 + i], refs[10].at[i]) for i in range(5)
+    ]
+    for store in stores:
+        store.start()
     for store in stores:
         store.wait()
 
@@ -413,8 +426,9 @@
     vm = pltpu.VMEM
     dma = pltpu.SemaphoreType.DMA
     anywhere = pl.BlockSpec(memory_space=pl.ANY)
-    inside = pl.BlockSpec(memory_space=pltpu.VMEM)
     scratch = [
+        vm((T, W), BF16), vm((T, W), BF16), vm((16, 16, W), BF16), vm((16, 16, W), BF16),
+        vm((W, W), F32), vm((W, W), F32), vm((1, W), F32),
         vm((128, T, T), BF16), vm((16, T, 16 * T), BF16),
         vm((8, 16), jnp.int32), vm((1, 16), jnp.int32), vm((16, T), jnp.int32),
         pltpu.SMEM((16, T), jnp.int32),
@@ -430,24 +444,25 @@
         vm((W + 16, W), BF16), vm((W + 16, W), BF16),
         vm((16, 32, W), BF16), vm((16, 32, W), BF16),
         vm((32, W), BF16), vm((8, 32, W), BF16),
-        dma((11,)), dma((2, 8)), dma((2, 8)), dma((2, 7)), dma((2, 7)),
+        dma((16,)), dma((2, 8)), dma((2, 8)), dma((2, 7)), dma((2, 7)),
         dma((2, 4, 3)), dma((2, 4, 3)), dma((2, 3)), dma((2, 3)),
         dma((2, 3)), dma((2, 3)), dma((2, 4, 3)), dma((2, 4, 3)),
         dma((2, 4)), dma((2, 4)), dma((2, 7)), dma((2, 7)),
         dma(()), dma(()), dma((15,)), dma((15,)), dma((7,)), dma((7,)),
         dma((15,)), dma((15,)), dma(()), dma(()),
     ]
+    shapes = (
+        jax.ShapeDtypeStruct((T, W), BF16),
+        jax.ShapeDtypeStruct((T, W), BF16),
+        jax.ShapeDtypeStruct((W, W), F32),
+        jax.ShapeDtypeStruct((W, W), F32),
+        jax.ShapeDtypeStruct((1, W), F32),
+    )
     raw = pl.pallas_call(
         kernel,
-        out_shape=(
-            jax.ShapeDtypeStruct((T, W), BF16),
-            jax.ShapeDtypeStruct((T, W), BF16),
-            jax.ShapeDtypeStruct((16, 16, W), BF16),
-            jax.ShapeDtypeStruct((16, 16, W), BF16),
-            jax.ShapeDtypeStruct((1, W), F32),
-        ),
+        out_shape=shapes,
         in_specs=[anywhere] * 9,
-        out_specs=[inside] * 5,
+        out_specs=[anywhere] * 5,
         scratch_shapes=scratch,
         compiler_params=pltpu.CompilerParams(
             collective_id=0, has_side_effects=True, vmem_limit_bytes=58 * 2**20
@@ -466,16 +481,10 @@
     )
     output, grad_features, self_grad, neigh_grad, bias_grad = pl.pallas_call(
         finish,
-        out_shape=(
-            jax.ShapeDtypeStruct((T, W), BF16),
-            jax.ShapeDtypeStruct((T, W), BF16),
-            jax.ShapeDtypeStruct((W, W), F32),
-            jax.ShapeDtypeStruct((W, W), F32),
-            jax.ShapeDtypeStruct((1, W), F32),
-        ),
-        in_specs=[inside] * 5,
+        out_shape=shapes,
+        in_specs=[pl.BlockSpec(memory_space=pltpu.VMEM)] * 5,
         out_specs=[anywhere] * 5,
-        scratch_shapes=[vm((W, W), F32), vm((W, W), F32), dma((5,))],
+        scratch_shapes=[dma((5,))],
         compiler_params=pltpu.CompilerParams(vmem_limit_bytes=62 * 2**20),
         name="finish",
     )(*raw)

time: 67.8 us -> 66.3 us (0.978)
  Pallas kernels: 67 us -> 65.6 us
    pallas_call x2, Pallas kernels: 67 us -> 65.6 us  [the longest x1 63.6 us: local(): pl.pallas_call(kernel, out_shape=shapes, in_specs=[anywhere] * 9, out_spe...]
where the time goes in v4:
time: 66.3 us; the launch traced here: 66.2 us
  Pallas kernels  65.6 us (99%)
    pallas_call x1, Pallas kernels, local(): pl.pallas_call(kernel, out_shape=shapes, in_specs=[anywhere] * 9, out_spe...  63.6 us
    pallas_call x1, Pallas kernels, local(): pl.pallas_call(finish, out_shape=shapes, in_specs=[pl.BlockSpec(memory_sp...  1.98 us

profile of v4, /device:TPU:1, one launch (start us, length us, event | category | flops | bytes accessed | tf_op | source)
XLA Modules:
  0.0 66.2 jit_solution(6946702693556925972)
XLA Ops:
  0.6 63.6 %sage.1 = (bf16[128,256]{1,0:T(8,128)(2,1)}, bf16[128,256]{1,0:T(8,128)(2,1)}, f32[256,256]{1,0:T(8,128)}, f32[256,256]{1,0:T(8,128)}, f32[1,256]{1,0:T(1,128)}) custom-call(bf16[128,256]{1,0:T(8,128)(2,1)} %feats_h.1, s32[1,128]{1,0:T(1,128)} %bitcast.11, bf16[128,128,128]{2,1,0:T(8,128)(2,1)} %bitcast.8, s32[8,16]{1,0:T(8,128)} %bitcast.9, ...), custom_call_target="tpu_custom_call" | custom-call | tf_op jit(solution)/shard_map/sage/pallas_call | solution.py:461
  64.2 2.0 %finish.1 = (bf16[128,256]{1,0:T(8,128)(2,1)}, bf16[128,256]{1,0:T(8,128)(2,1)}, f32[256,256]{1,0:T(8,128)}, f32[256,256]{1,0:T(8,128)}, f32[1,256]{1,0:T(1,128)}) custom-call(bf16[128,256]{1,0:T(8,128)(2,1)} %get-tuple-element.15.refs_0_, bf16[128,256]{1,0:T(8,128)(2,1)} %get-tuple-element.16.refs_1_, f32[256,256]{1,0:T(8,128)} %get-tuple-element.17.refs_2_, ...), custom_call_target="tpu_custom_call" | custom-call | tf_op jit(solution)/shard_map/finish/pallas_call | solution.py:482

commit v5 on v4

--- a/solution.py
+++ b/solution.py
@@ -14,7 +14,7 @@
 W = 256
 CHIPS = [(dx, dz) for dx in (2, 1, 3, 0) for dz in (1, 0) if dx or dz]
 PLANE = [(dx, dy) for dx in range(4) for dy in range(4) if dx or dy]
-FAR = (2, 1, 3)
+FAR = (1, 3, 2)
 FAR_FIRST = (2, 1, 3, 0)
 GELU_C = 0.7978845608028654
 
@@ -83,7 +83,7 @@
         for zz in [(z + d) % 8 for d in range(1, 8)]
     ]
     barrier = pltpu.get_barrier_semaphore()
-    for partner in partners:
+    for partner in reversed(partners):
         pl.semaphore_signal(barrier, inc=1, device_id=partner, device_id_type=MESH)
 
     halves = [feats_h.at[:, pl.ds(h * T, T)] for h in range(2)]
@@ -166,7 +166,7 @@
 
     for h in range(2):
         forwards = []
-        for j in (4, 1, 3, 5, 6, 0, 2):
+        for j in (6, 3, 5, 1, 2, 4, 0):
             dx, dz = CHIPS[j]
             a_sent[h][j].wait_recv()
             piece = feats_all.at[h, piece_at(*chip(-dx, dz), c)]
@@ -283,7 +283,7 @@
     ar2_r[spot] = ar2_s[spot]
 
     for h in range(2):
-        for k in (1, 2, 0):
+        for k in range(3):
             cz_sent[h][k].wait_recv()
             piece = grads_all.at[h, ((zh - FAR[k]) % 4) * 4 + y]
             for m, dy in enumerate(FAR):

time: 66.3 us -> 65.9 us (level)
  no operation moved by 1% of the time
where the time goes in v5:
time: 65.9 us; the launch traced here: 65.8 us
  Pallas kernels  65.1 us (99%)
    pallas_call x1, Pallas kernels, local(): pl.pallas_call(kernel, out_shape=shapes, in_specs=[anywhere] * 9, out_spe...  63.1 us
    pallas_call x1, Pallas kernels, local(): pl.pallas_call(finish, out_shape=shapes, in_specs=[pl.BlockSpec(memory_sp...  1.98 us

profile of v5, /device:TPU:1, one launch (start us, length us, event | category | flops | bytes accessed | tf_op | source)
XLA Modules:
  0.0 65.8 jit_solution(2506693876685132446)
XLA Ops:
  0.6 63.1 %sage.1 = (bf16[128,256]{1,0:T(8,128)(2,1)}, bf16[128,256]{1,0:T(8,128)(2,1)}, f32[256,256]{1,0:T(8,128)}, f32[256,256]{1,0:T(8,128)}, f32[1,256]{1,0:T(1,128)}) custom-call(bf16[128,256]{1,0:T(8,128)(2,1)} %feats_h.1, s32[1,128]{1,0:T(1,128)} %bitcast.11, bf16[128,128,128]{2,1,0:T(8,128)(2,1)} %bitcast.8, s32[8,16]{1,0:T(8,128)} %bitcast.9, ...), custom_call_target="tpu_custom_call" | custom-call | tf_op jit(solution)/shard_map/sage/pallas_call | solution.py:461
  63.8 2.0 %finish.1 = (bf16[128,256]{1,0:T(8,128)(2,1)}, bf16[128,256]{1,0:T(8,128)(2,1)}, f32[256,256]{1,0:T(8,128)}, f32[256,256]{1,0:T(8,128)}, f32[1,256]{1,0:T(1,128)}) custom-call(bf16[128,256]{1,0:T(8,128)(2,1)} %get-tuple-element.15.refs_0_, bf16[128,256]{1,0:T(8,128)(2,1)} %get-tuple-element.16.refs_1_, f32[256,256]{1,0:T(8,128)} %get-tuple-element.17.refs_2_, ...), custom_call_target="tpu_custom_call" | custom-call | tf_op jit(solution)/shard_map/finish/pallas_call | solution.py:482

commit v6 on v5

--- a/solution.py
+++ b/solution.py
@@ -270,6 +270,19 @@
     mine = ar1_s[W : W + 16].astype(F32)
     both = jnp.sum(mine + other, axis=0, keepdims=True)
     ar2_s[:, 16:32] = jnp.broadcast_to(bias_block(both)[None], (16, 16, W))
+    def pass_along(h):
+        for k in range(3):
+            cz_sent[h][k].wait_recv()
+            piece = grads_all.at[h, ((zh - FAR[k]) % 4) * 4 + y]
+            for m, dy in enumerate(FAR):
+                cy_sent[h].append(
+                    send(
+                        piece, piece, cy_ss.at[h, k, m], cy_rs.at[h, k, m],
+                        device(x, zl, c, (y + dy) % 4, zh),
+                    )
+                )
+
+    pass_along(0)
     spot = x * 4 + y
     r2 = []
     for j, (dx, dy) in enumerate(PLANE):
@@ -281,18 +294,7 @@
             )
         )
     ar2_r[spot] = ar2_s[spot]
-
-    for h in range(2):
-        for k in range(3):
-            cz_sent[h][k].wait_recv()
-            piece = grads_all.at[h, ((zh - FAR[k]) % 4) * 4 + y]
-            for m, dy in enumerate(FAR):
-                cy_sent[h].append(
-                    send(
-                        piece, piece, cy_ss.at[h, k, m], cy_rs.at[h, k, m],
-                        device(x, zl, c, (y + dy) % 4, zh),
-                    )
-                )
+    pass_along(1)
 
     for copy in r2:
         copy.wait_recv()

time: 65.9 us -> 68 us (1.032)
  Pallas kernels: 65.1 us -> 67.2 us
    pallas_call x1, Pallas kernels: 63.1 us -> 65.2 us  [local(): pl.pallas_call(kernel, out_shape=shapes, in_specs=[anywhere] * 9, out_spe...]
where the time goes in v6:
time: 68 us; the launch traced here: 67.9 us
  Pallas kernels  67.2 us (99%)
    pallas_call x1, Pallas kernels, local(): pl.pallas_call(kernel, out_shape=shapes, in_specs=[anywhere] * 9, out_spe...  65.2 us
    pallas_call x1, Pallas kernels, local(): pl.pallas_call(finish, out_shape=shapes, in_specs=[pl.BlockSpec(memory_sp...  1.98 us

profile of v6, /device:TPU:1, one launch (start us, length us, event | category | flops | bytes accessed | tf_op | source)
XLA Modules:
  0.0 67.9 jit_solution(5051719274872830816)
XLA Ops:
  0.6 65.2 %sage.1 = (bf16[128,256]{1,0:T(8,128)(2,1)}, bf16[128,256]{1,0:T(8,128)(2,1)}, f32[256,256]{1,0:T(8,128)}, f32[256,256]{1,0:T(8,128)}, f32[1,256]{1,0:T(1,128)}) custom-call(bf16[128,256]{1,0:T(8,128)(2,1)} %feats_h.1, s32[1,128]{1,0:T(1,128)} %bitcast.11, bf16[128,128,128]{2,1,0:T(8,128)(2,1)} %bitcast.8, s32[8,16]{1,0:T(8,128)} %bitcast.9, ...), custom_call_target="tpu_custom_call" | custom-call | tf_op jit(solution)/shard_map/sage/pallas_call | solution.py:463
  65.9 2.0 %finish.1 = (bf16[128,256]{1,0:T(8,128)(2,1)}, bf16[128,256]{1,0:T(8,128)(2,1)}, f32[256,256]{1,0:T(8,128)}, f32[256,256]{1,0:T(8,128)}, f32[1,256]{1,0:T(1,128)}) custom-call(bf16[128,256]{1,0:T(8,128)(2,1)} %get-tuple-element.15.refs_0_, bf16[128,256]{1,0:T(8,128)(2,1)} %get-tuple-element.16.refs_1_, f32[256,256]{1,0:T(8,128)} %get-tuple-element.17.refs_2_, ...), custom_call_target="tpu_custom_call" | custom-call | tf_op jit(solution)/shard_map/finish/pallas_call | solution.py:484
